TPU v7x, 32 devices: a whole 2x2x4 slice. The times are simulated.
32 devices in a mesh: group: 2 (over y), section: 4 (over z), dp: 4 (over x, core).
Axes of the slice: x: 2, y: 2, z: 4, core: 2. Of those that a mesh axis runs over, the one named last changes fastest.
Arguments:
- tokens: bfloat16 [4, 8, 32, 1600], P(None, ('group', 'dp')), parts along dimension 1, may hold values from -6 to 6
- pixel_index: int32 [4, 8, 384], P(None, ('group', 'dp')), parts along dimension 1, may hold values from 0 to 6271
- point_mask: int32 [4, 8, 384], P(None, ('group', 'dp')), parts along dimension 1, may hold values from 0 to 1, as said below
- point_depth: float32 [4, 8, 384], P(None, ('group', 'dp')), parts along dimension 1, may hold values from -6 to 6
- hook_section: int32 [4], replicated, may hold values from 0 to 2, as said below
- w_query: bfloat16 [4, 1600, 832], P('section')
- w_key: bfloat16 [4, 1600, 832], P('section')
- w_value: bfloat16 [4, 1600, 832], P('section'), may hold values from -0.15625 to 0.15625
- w_output: bfloat16 [4, 832, 1600], P('section'), may hold values from -0.21875 to 0.21875
- reassemble: bfloat16 [5, 1600, 128], P(None, None, ('section', 'dp')), may hold values from -0.15625 to 0.15625
- merging: bfloat16 [4, 128, 128], P(None, None, ('section', 'dp')), may hold values from -0.5 to 0.5
- predict: bfloat16 [128, 196], P(('section', 'dp')), may hold values from -0.5 to 0.5
Outputs:
- grad_query: bfloat16 [8, 1600, 832], P(('group', 'section'), 'dp'), parts along dimension 0
- grad_key: bfloat16 [8, 1600, 832], P(('group', 'section'), 'dp'), parts along dimension 0
- grad_value: bfloat16 [8, 1600, 832], P(('group', 'section'), 'dp'), parts along dimension 0
- grad_output: bfloat16 [8, 832, 1600], P(('group', 'section'), 'dp'), parts along dimension 0
- grad_reassemble: float32 [10, 1600, 128], P('group', None, ('section', 'dp')), parts along dimension 0
- grad_merging: float32 [8, 128, 128], P('group', None, ('section', 'dp')), parts along dimension 0
- grad_predict: float32 [256, 196], P(('group', 'section', 'dp')), parts along dimension 0
There are 2 independent parts, one for each index of `group`. A program takes and returns all parts, laid end to end along the dimension named above; an argument that names none is the same for every part. Nothing has to cross between parts.
Inputs may be any that keep to these rules, and one draw needn't show every extreme that they name: `point_mask`: in each image the valid points come first, and at least 48 of them are valid. `hook_section`: Sorted; the last entry is 2.
All inputs are finite; a program needn't handle non-finite values.
Results may differ from a plain program's by a relative error of at most 0.03.
Values may be sent and summed in bfloat16 or wider, within the bound.
A program may use at most 128 MiB of HBM per device.

v0:
```python
import math
import jax
import jax.numpy as jnp
from jax import lax
from jax.sharding import PartitionSpec as P

HEADS = 13
NHOOK = 4
EPS = 1e-06


def passed_along(block, axis, distance):
    devices = range(lax.axis_size(axis))
    route = [(i - distance, i) for i in devices if i - distance in devices]
    return lax.ppermute(block, axis, route)


def broadcast(value, axis, source):
    kept = jnp.where(lax.axis_index(axis) == source, value, 0).astype(value.dtype)
    return lax.psum(kept, axis)


def as_sent(x):
    return jax.tree.map(lambda a: a.astype(jnp.bfloat16) if a.dtype == jnp.float32 else a, x)


def rms_normed(stream):
    widened = stream.astype(jnp.float32)
    inv_root = lax.rsqrt(jnp.mean(widened * widened, axis=-1, keepdims=True) + EPS)
    return (widened * inv_root).astype(jnp.bfloat16)


def attend(query_rows, key_rows, value_rows):
    image_count, token_count, inner_width = query_rows.shape
    head_width = inner_width // HEADS
    shape_heads = (image_count, token_count, HEADS, head_width)
    query_heads = query_rows.astype(jnp.float32).reshape(shape_heads)
    key_heads = key_rows.astype(jnp.float32).reshape(shape_heads)
    value_heads = value_rows.astype(jnp.float32).reshape(shape_heads)
    scores = jnp.einsum("bqhe,bkhe->bhqk", query_heads, key_heads) / math.sqrt(head_width)
    probabilities = jax.nn.softmax(scores, axis=-1).astype(jnp.bfloat16)
    mixed_heads = jnp.einsum("bhqk,bkhe->bqhe", probabilities.astype(jnp.float32), value_heads)
    return mixed_heads.reshape(image_count, token_count, inner_width).astype(jnp.bfloat16)


def attention_layer(stream, layer_query, layer_key, layer_value, layer_output, nudges):
    image_count, token_count, model_width = stream.shape
    normed = rms_normed(stream).reshape(image_count * token_count, model_width)
    query_rows = (
        jnp.dot(normed, layer_query, preferred_element_type=jnp.float32).astype(jnp.bfloat16)
        + nudges[0]
    )
    key_rows = (
        jnp.dot(normed, layer_key, preferred_element_type=jnp.float32).astype(jnp.bfloat16)
        + nudges[1]
    )
    value_rows = (
        jnp.dot(normed, layer_value, preferred_element_type=jnp.float32).astype(jnp.bfloat16)
        + nudges[2]
    )
    inner_width = layer_query.shape[1]
    mixed = attend(
        query_rows.reshape(image_count, token_count, inner_width),
        key_rows.reshape(image_count, token_count, inner_width),
        value_rows.reshape(image_count, token_count, inner_width),
    )
    mixed_rows = mixed.reshape(image_count * token_count, inner_width)
    update = jnp.dot(mixed_rows, layer_output, preferred_element_type=jnp.float32)
    update = update.reshape(image_count, token_count, model_width)
    output_rows = stream.astype(jnp.float32) + update
    return (output_rows, (normed, mixed_rows))


def reassemble_map(features, weight):
    flat_rows = features.reshape(-1, features.shape[-1]).astype(jnp.bfloat16)
    return jnp.dot(flat_rows, weight, preferred_element_type=jnp.float32).astype(jnp.bfloat16)


def head_rest(projected, top_projected, merging, predict, pixel_index, point_mask, point_depth):
    merged = top_projected.astype(jnp.float32)
    for hook_slot in range(len(projected) - 1, -1, -1):
        activated = jax.nn.silu(merged).astype(jnp.bfloat16)
        merged = projected[hook_slot].astype(jnp.float32) + jnp.dot(
            activated, merging[hook_slot], preferred_element_type=jnp.float32
        )
    activated = jax.nn.silu(merged).astype(jnp.bfloat16)
    depth_rows = jnp.dot(activated, predict, preferred_element_type=jnp.float32)
    depth_map = depth_rows.reshape(pixel_index.shape[0], pixel_index.shape[1], -1)
    picked = jnp.take_along_axis(depth_map, pixel_index, axis=2)
    valid_mask = point_mask.astype(jnp.float32)
    valid_count = jnp.sum(valid_mask, axis=2)
    misfit = (picked - point_depth) * valid_mask
    return jnp.sum(jnp.sum(misfit * misfit, axis=2) / valid_count)


def keep_rows(stream):
    return stream


def put_slot(store_array, item_rows, micro_slot, active):
    updated = lax.dynamic_update_index_in_dim(store_array, item_rows, micro_slot, 0)
    return jnp.where(active, updated, store_array)


def contract(left_rows, right_rows):
    return jnp.einsum("mrd,mrh->dh", left_rows, right_rows, preferred_element_type=jnp.float32)


def on_device(
    tokens,
    pixel_index,
    point_mask,
    point_depth,
    hook_section,
    w_query,
    w_key,
    w_value,
    w_output,
    reassemble,
    merging,
    predict,
):
    section_index = lax.axis_index("section")
    section_count = lax.axis_size("section")
    last_section = section_count - 1
    is_last = section_index == last_section
    micro_count = tokens.shape[0]
    token_rows = tokens.shape[1] * tokens.shape[2]
    model_width = tokens.shape[3]
    inner_width = w_query.shape[2]
    layer_query = w_query[0]
    layer_key = w_key[0]
    layer_value = w_value[0]
    layer_output = w_output[0]
    full_reassemble, full_merging, full_predict = (
        lax.all_gather(reassemble, ("section", "dp"), axis=2, tiled=True),
        lax.all_gather(merging, ("section", "dp"), axis=2, tiled=True),
        lax.all_gather(predict, ("section", "dp"), axis=0, tiled=True),
    )
    zero_nudges = jnp.zeros((3, token_rows, inner_width), jnp.bfloat16)
    zero_rows = jnp.zeros(tokens.shape[1:], jnp.float32)
    empty_store = jnp.zeros(tokens.shape, jnp.float32)

    def run_layer(stream):
        return attention_layer(
            stream, layer_query, layer_key, layer_value, layer_output, zero_nudges
        )[0]

    def forward_step(time_step, carried):
        incoming, inputs_store, outputs_store = carried
        micro_index = time_step - section_index
        active = jnp.logical_and(micro_index >= 0, micro_index < micro_count)
        micro_slot = jnp.clip(micro_index, 0, micro_count - 1)
        fresh_rows = lax.dynamic_index_in_dim(tokens, micro_slot, 0, keepdims=False).astype(
            jnp.float32
        )
        source = jnp.where(section_index == 0, fresh_rows, incoming)
        result = lax.cond(active, run_layer, keep_rows, source)
        inputs_store = put_slot(inputs_store, source, micro_slot, active)
        outputs_store = put_slot(outputs_store, result, micro_slot, active)
        incoming = passed_along(result, "section", 1)
        return (incoming, inputs_store, outputs_store)

    unused, inputs_store, outputs_store = lax.fori_loop(
        0, micro_count + section_count - 1, forward_step, (zero_rows, empty_store, empty_store)
    )
    hook_sum = jnp.zeros(tokens.shape, jnp.float32)
    received = []
    for hook_slot in range(NHOOK):
        local_piece = reassemble_map(outputs_store, full_reassemble[hook_slot])
        received.append(broadcast(local_piece, "section", hook_section[hook_slot]))
    projected_in = tuple(received)

    def head_grads(head_items):

        def loss_terms(projected, top_feature, reassemble_last, head_merging, head_predict):
            top_projected = reassemble_map(top_feature, reassemble_last)
            return head_rest(
                projected,
                top_projected,
                head_merging,
                head_predict,
                pixel_index,
                point_mask,
                point_depth,
            )

        loss_value, pullback = jax.vjp(
            loss_terms,
            head_items[0],
            head_items[1],
            full_reassemble[NHOOK],
            full_merging,
            full_predict,
        )
        return pullback(jnp.ones((), jnp.float32))

    def no_grads(head_items):
        return (
            tuple((jnp.zeros_like(array_item) for array_item in head_items[0])),
            jnp.zeros_like(head_items[1]),
            jnp.zeros_like(full_reassemble[NHOOK]),
            jnp.zeros_like(full_merging),
            jnp.zeros_like(full_predict),
        )

    projected_grads, last_grad, reassemble_last_grad, grad_merging, grad_predict = lax.cond(
        is_last, head_grads, no_grads, (projected_in, outputs_store)
    )
    projected_cotangents = broadcast(jnp.stack(projected_grads), "section", last_section)
    weight_grads = []
    for hook_slot in range(NHOOK):
        unused_rows, pullback = jax.vjp(reassemble_map, outputs_store, full_reassemble[hook_slot])
        feature_grad, weight_grad = pullback(projected_cotangents[hook_slot])
        is_owner = hook_section[hook_slot] == section_index
        hook_sum = hook_sum + jnp.where(is_owner, feature_grad, 0.0)
        weight_grads.append(jnp.where(is_owner, weight_grad, jnp.zeros_like(weight_grad)))
    weight_grads.append(reassemble_last_grad)
    grad_reassemble = jnp.stack(weight_grads)
    hook_grad = hook_sum

    def backward_one(stream, cotangent):

        def local_layer(entry_rows, nudges):
            return attention_layer(
                entry_rows, layer_query, layer_key, layer_value, layer_output, nudges
            )

        unused_rows, pullback, saved = jax.vjp(local_layer, stream, zero_nudges, has_aux=True)
        entry_grad, nudge_grad = pullback(cotangent)
        return (entry_grad, nudge_grad, saved[0], saved[1])

    def skip_one(stream, cotangent):
        return (
            jnp.zeros_like(stream),
            zero_nudges,
            jnp.zeros((token_rows, model_width), jnp.bfloat16),
            jnp.zeros((token_rows, inner_width), jnp.bfloat16),
        )

    def backward_step(time_step, carried):
        incoming, nudge_store, normed_store, mixed_store, cotangent_store = carried
        micro_index = time_step - (last_section - section_index)
        active = jnp.logical_and(micro_index >= 0, micro_index < micro_count)
        micro_slot = jnp.clip(micro_index, 0, micro_count - 1)
        upstream = jnp.where(
            is_last, lax.dynamic_index_in_dim(last_grad, micro_slot, 0, keepdims=False), incoming
        )
        cotangent = upstream + lax.dynamic_index_in_dim(hook_grad, micro_slot, 0, keepdims=False)
        stream = lax.dynamic_index_in_dim(inputs_store, micro_slot, 0, keepdims=False)
        entry_grad, nudge_grad, normed, mixed_rows = lax.cond(
            active, backward_one, skip_one, stream, cotangent
        )
        nudge_store = put_slot(nudge_store, nudge_grad, micro_slot, active)
        normed_store = put_slot(normed_store, normed, micro_slot, active)
        mixed_store = put_slot(mixed_store, mixed_rows, micro_slot, active)
        cotangent_store = put_slot(cotangent_store, cotangent, micro_slot, active)
        incoming = jax.tree.map(
            lambda part, own: part.astype(own.dtype),
            passed_along(as_sent(entry_grad), "section", -1),
            entry_grad,
        )
        return (incoming, nudge_store, normed_store, mixed_store, cotangent_store)

    start_state = (
        zero_rows,
        jnp.zeros((micro_count, 3, token_rows, inner_width), jnp.bfloat16),
        jnp.zeros((micro_count, token_rows, model_width), jnp.bfloat16),
        jnp.zeros((micro_count, token_rows, inner_width), jnp.bfloat16),
        empty_store,
    )
    unused, nudge_store, normed_store, mixed_store, cotangent_store = lax.fori_loop(
        0, micro_count + section_count - 1, backward_step, start_state
    )
    grad_query = contract(normed_store, nudge_store[:, 0])
    grad_key = contract(normed_store, nudge_store[:, 1])
    grad_value = contract(normed_store, nudge_store[:, 2])
    mixed_all = mixed_store.reshape(micro_count * token_rows, inner_width)
    update_grad = cotangent_store.reshape(micro_count * token_rows, model_width)

    def output_map(weight):
        return jnp.dot(mixed_all, weight, preferred_element_type=jnp.float32)

    unused_update, output_pullback = jax.vjp(output_map, layer_output)
    grad_output = output_pullback(update_grad)[0].astype(jnp.float32)
    summed_query, summed_key, summed_value, summed_output = (
        lax.psum_scatter(
            grad_query[None].astype(jnp.bfloat16), "dp", scatter_dimension=1, tiled=True
        ).astype(jnp.float32),
        lax.psum_scatter(
            grad_key[None].astype(jnp.bfloat16), "dp", scatter_dimension=1, tiled=True
        ).astype(jnp.float32),
        lax.psum_scatter(
            grad_value[None].astype(jnp.bfloat16), "dp", scatter_dimension=1, tiled=True
        ).astype(jnp.float32),
        lax.psum_scatter(
            grad_output[None].astype(jnp.bfloat16), "dp", scatter_dimension=1, tiled=True
        ).astype(jnp.float32),
    )
    head_reassemble, head_merging, head_predict = (
        lax.psum_scatter(
            grad_reassemble.astype(jnp.float32), ("section", "dp"), scatter_dimension=2, tiled=True
        ),
        lax.psum_scatter(
            grad_merging.astype(jnp.float32), ("section", "dp"), scatter_dimension=2, tiled=True
        ),
        lax.psum_scatter(
            grad_predict.astype(jnp.float32), ("section", "dp"), scatter_dimension=0, tiled=True
        ),
    )
    return (
        summed_query.astype(jnp.bfloat16),
        summed_key.astype(jnp.bfloat16),
        summed_value.astype(jnp.bfloat16),
        summed_output.astype(jnp.bfloat16),
        head_reassemble,
        head_merging,
        head_predict,
    )


def solution(mesh):
    placed = (
        P(None, ("group", "dp"), None, None),
        P(None, ("group", "dp"), None),
        P(None, ("group", "dp"), None),
        P(None, ("group", "dp"), None),
        P(),
        P("section", None, None),
        P("section", None, None),
        P("section", None, None),
        P("section", None, None),
        P(None, None, ("section", "dp")),
        P(None, None, ("section", "dp")),
        P(("section", "dp"), None),
    )
    return jax.shard_map(
        on_device,
        mesh=mesh,
        in_specs=placed,
        out_specs=(
            P(("group", "section"), "dp", None),
            P(("group", "section"), "dp", None),
            P(("group", "section"), "dp", None),
            P(("group", "section"), "dp", None),
            P("group", None, ("section", "dp")),
            P("group", None, ("section", "dp")),
            P(("group", "section", "dp"), None),
        ),
        check_vma=False,
    )
```

profile of v0, /device:TPU:0, one launch (start us, length us, event | category | flops | bytes accessed | tf_op | source)
XLA Modules:
  0.0 981.0 jit_solution(7728629565180497052)
XLA Ops:
  14.5 4.3 copy.215
  18.8 5.3 copy.216
  24.1 5.3 copy.214
  30.4 131.4 %while.42 = (s32[]{:T(128)}, f32[1,32,1600]{2,1,0:T(8,128)S(1)}, f32[4,1,32,1600]{3,2,1,0:T(8,128)}, bf16[4,1,32,1600]{3,2,1,0:T(8,128)(2,1)}, s32[]{:T(128)}, /...) while((s32[]{:T(128)}, f32[1,32,1600]{2,1,0:T(8,128)S(1)}, ...), condition=%wide.region_6.7_spmd, body=%wide.region_0.6_spmd.sunk | while | flops 344828992 | bytes 25776712 | solution.py:164
  32.1 10.4 %conditional.7 = (f32[1,32,1600]{2,1,0:T(8,128)S(1)}) conditional(s32[]{:T(128)} %convert_element_type.778, f32[1,32,1600]{2,1,0:T(8,128)S(1)} %get-tuple-element.1149, (f32[1,32,1600]{2,1,0:T(8,128)S(1)}, bf16[1600,832]{1,0:T(8,128)(2,1)}, bf16[1600,832]{1,0:T(8,128)(2,1)S(1)}, bf16[1600,832]{1,0:T(8,128)(2,1)}, bf16[832,1600]{1,0:T(8,128)(2,1)}) %tuple.167), branch_computations={%region_1.1_spmd, %region_2.5_spmd} | conditional | flops 344624192 | bytes 23596836 | solution.py:158
  32.3 2.5 convolution_convert_fusion.1
  40.2 2.3 fusion.1
  45.4 7.6 collective-permute-done
  54.7 10.4 %conditional.7 = (f32[1,32,1600]{2,1,0:T(8,128)S(1)}) conditional(s32[]{:T(128)} %convert_element_type.778, f32[1,32,1600]{2,1,0:T(8,128)S(1)} %get-tuple-element.1149, (f32[1,32,1600]{2,1,0:T(8,128)S(1)}, bf16[1600,832]{1,0:T(8,128)(2,1)}, bf16[1600,832]{1,0:T(8,128)(2,1)S(1)}, bf16[1600,832]{1,0:T(8,128)(2,1)}, bf16[832,1600]{1,0:T(8,128)(2,1)}) %tuple.167), branch_computations={%region_1.1_spmd, %region_2.5_spmd} | conditional | flops 344624192 | bytes 23596836 | solution.py:158
  55.0 2.5 convolution_convert_fusion.1
  62.8 2.3 fusion.1
  65.1 4.4 collective-permute-start
  71.1 3.2 collective-permute-done
  76.0 10.4 %conditional.7 = (f32[1,32,1600]{2,1,0:T(8,128)S(1)}) conditional(s32[]{:T(128)} %convert_element_type.778, f32[1,32,1600]{2,1,0:T(8,128)S(1)} %get-tuple-element.1149, (f32[1,32,1600]{2,1,0:T(8,128)S(1)}, bf16[1600,832]{1,0:T(8,128)(2,1)}, bf16[1600,832]{1,0:T(8,128)(2,1)S(1)}, bf16[1600,832]{1,0:T(8,128)(2,1)}, bf16[832,1600]{1,0:T(8,128)(2,1)}) %tuple.167), branch_computations={%region_1.1_spmd, %region_2.5_spmd} | conditional | flops 344624192 | bytes 23596836 | solution.py:158
  76.2 2.5 convolution_convert_fusion.1
  84.1 2.3 fusion.1
  86.4 4.4 collective-permute-start
  92.3 2.3 collective-permute-done
  96.4 10.4 %conditional.7 = (f32[1,32,1600]{2,1,0:T(8,128)S(1)}) conditional(s32[]{:T(128)} %convert_element_type.778, f32[1,32,1600]{2,1,0:T(8,128)S(1)} %get-tuple-element.1149, (f32[1,32,1600]{2,1,0:T(8,128)S(1)}, bf16[1600,832]{1,0:T(8,128)(2,1)}, bf16[1600,832]{1,0:T(8,128)(2,1)S(1)}, bf16[1600,832]{1,0:T(8,128)(2,1)}, bf16[832,1600]{1,0:T(8,128)(2,1)}) %tuple.167), branch_computations={%region_1.1_spmd, %region_2.5_spmd} | conditional | flops 344624192 | bytes 23596836 | solution.py:158
  96.6 2.5 convolution_convert_fusion.1
  104.5 2.3 fusion.1
  106.8 4.4 collective-permute-start
  116.2 14.8 %collective-permute-start = (f32[1,32,1600]{2,1,0:T(8,128)S(1)}, f32[1,32,1600]{2,1,0:T(8,128)S(1)}, u32[]{:S(2)}, u32[]{:S(2)}) collective-permute-start(f32[1,32,1600]{2,1,0:T(8,128)S(1)} %get-tuple-element.1302), channel_id=1, source_target_pairs={{0,4},{4,8},{8,12},{1,5},{5,9},{9,13},{2,6},{6,10},{10,14},{3,7},{... | collective-permute-start | bytes 614408 | tf_op jit(solution)/shard_map/while/body/eval_jaxpr/ppermute | solution.py:15
  136.1 4.4 collective-permute-start
  145.5 12.9 %collective-permute-start = (f32[1,32,1600]{2,1,0:T(8,128)S(1)}, f32[1,32,1600]{2,1,0:T(8,128)S(1)}, u32[]{:S(2)}, u32[]{:S(2)}) collective-permute-start(f32[1,32,1600]{2,1,0:T(8,128)S(1)} %get-tuple-element.1302), channel_id=1, source_target_pairs={{0,4},{4,8},{8,12},{1,5},{5,9},{9,13},{2,6},{6,10},{10,14},{3,7},{... | collective-permute-start | bytes 614408 | tf_op jit(solution)/shard_map/while/body/eval_jaxpr/ppermute | solution.py:15
  170.1 31.5 %all_gather.11 = bf16[128,196]{1,0:T(8,128)(2,1)S(1)} all-gather(bf16[8,196]{1,0:T(8,128)(2,1)S(1)} %copy-done.20), channel_id=1, replica_groups=mesh['group'=2,'section'=4,'dp'=4] {'section','dp'}, dimensions={0}, use_global_device_ids=true | all-gather | bytes 53312 | tf_op jit(solution)/shard_map/all_gather | solution.py:138
  201.6 17.9 %all_gather.10 = bf16[4,128,128]{1,0,2:T(4,128)(2,1)S(1)} all-gather(bf16[4,128,8]{1,0,2:T(4,128)(2,1)S(1)} %copy.217), channel_id=1, replica_groups=mesh['group'=2,'section'=4,'dp'=4] {'section','dp'}, dimensions={2}, use_global_device_ids=true | all-gather | bytes 139264 | tf_op jit(solution)/shard_map/all_gather | solution.py:137
  219.5 4.9 conditional.3
  228.7 75.9 %all-reduce.11.cloned.1.call-done = bf16[4,128,128]{2,1,0:T(8,128)(2,1)} async-done(((bf16[4,128,128]{2,1,0:T(8,128)(2,1)}), bf16[4,128,128]{2,1,0:T(8,128)(2,1)}) %all-reduce.11.cloned.1.call-update) | async-done | bytes 131088 | tf_op jit(solution)/shard_map/psum | solution.py:20
  308.6 2.3 fusion.96
  310.9 2.4 copy.223
  315.7 278.6 %while.43 = (s32[]{:T(128)}, f32[1,32,1600]{2,1,0:T(8,128)S(1)}, bf16[4,3,32,832]{3,2,0,1:T(8,128)(2,1)}, bf16[4,32,1600]{2,1,0:T(8,128)(2,1)}, bf16[4,32,832]{2...) while((s32[]{:T(128)}, f32[1,32,1600]{2,1,0:T(8,128)S(1)}, ...), condition=%wide.region_24.25_spmd.clone, body=%wide.region_16.24_spmd.clone.sunk | while | flops 608857152 | bytes 61259056 | solution.py:272
  344.9 87.1 %collective-permute-done.1 = bf16[1,32,1600]{2,1,0:T(8,128)(2,1)S(1)} collective-permute-done((bf16[1,32,1600]{2,1,0:T(8,128)(2,1)}, bf16[1,32,1600]{2,1,0:T(8,128)(2,1)S(1)}, u32[]{:S(2)}, u32[]{:S(2)}) %collective-permute-start.1) | collective-permute-done | bytes 102432 | tf_op jit(solution)/shard_map/while/body/eval_jaxpr/ppermute | solution.py:15
  433.8 31.3 %conditional.8 = (bf16[1,32,1600]{2,1,0:T(8,128)(2,1)}, bf16[1,3,32,832]{3,2,1,0:T(8,128)(2,1)S(1)}, bf16[1,32,1600]{2,1,0:T(8,128)(2,1)}, bf16[1,32,832]{2,1,0:T(8,128)(2,1)S(1)}) conditional(s32[]{:T(128)} %convert_element_type.779, () %tuple.170, (f32[1,32,1600]{2,1,0:T(8,128)S(1)}, bf16[832,1600]{1,0:T(8,128)(2,1)}, ...), branch_computations={%region_17.17_spmd, %region_18.23_spmd} | conditional | flops 608443456 | bytes 57541052 | solution.py:251
  435.0 2.5 convolution_convert_fusion.13
  458.3 2.9 convolution_convert_fusion.5
  461.3 2.1 fusion.36
  474.6 31.3 %conditional.8 = (bf16[1,32,1600]{2,1,0:T(8,128)(2,1)}, bf16[1,3,32,832]{3,2,1,0:T(8,128)(2,1)S(1)}, bf16[1,32,1600]{2,1,0:T(8,128)(2,1)}, bf16[1,32,832]{2,1,0:T(8,128)(2,1)S(1)}) conditional(s32[]{:T(128)} %convert_element_type.779, () %tuple.170, (f32[1,32,1600]{2,1,0:T(8,128)S(1)}, bf16[832,1600]{1,0:T(8,128)(2,1)}, ...), branch_computations={%region_17.17_spmd, %region_18.23_spmd} | conditional | flops 608443456 | bytes 57541052 | solution.py:251
  475.8 2.5 convolution_convert_fusion.13
  499.1 2.9 convolution_convert_fusion.5
  502.0 2.1 fusion.36
  515.3 31.3 %conditional.8 = (bf16[1,32,1600]{2,1,0:T(8,128)(2,1)}, bf16[1,3,32,832]{3,2,1,0:T(8,128)(2,1)S(1)}, bf16[1,32,1600]{2,1,0:T(8,128)(2,1)}, bf16[1,32,832]{2,1,0:T(8,128)(2,1)S(1)}) conditional(s32[]{:T(128)} %convert_element_type.779, () %tuple.170, (f32[1,32,1600]{2,1,0:T(8,128)S(1)}, bf16[832,1600]{1,0:T(8,128)(2,1)}, ...), branch_computations={%region_17.17_spmd, %region_18.23_spmd} | conditional | flops 608443456 | bytes 57541052 | solution.py:251
  516.5 2.5 convolution_convert_fusion.13
  539.8 2.9 convolution_convert_fusion.5
  542.7 2.1 fusion.36
  556.0 31.3 %conditional.8 = (bf16[1,32,1600]{2,1,0:T(8,128)(2,1)}, bf16[1,3,32,832]{3,2,1,0:T(8,128)(2,1)S(1)}, bf16[1,32,1600]{2,1,0:T(8,128)(2,1)}, bf16[1,32,832]{2,1,0:T(8,128)(2,1)S(1)}) conditional(s32[]{:T(128)} %convert_element_type.779, () %tuple.170, (f32[1,32,1600]{2,1,0:T(8,128)S(1)}, bf16[832,1600]{1,0:T(8,128)(2,1)}, ...), branch_computations={%region_17.17_spmd, %region_18.23_spmd} | conditional | flops 608443456 | bytes 57541052 | solution.py:251
  557.2 2.5 convolution_convert_fusion.13
  580.5 2.9 convolution_convert_fusion.5
  596.3 12.4 %copy.242 = bf16[1,1600,832]{2,0,1:T(2,128)(2,1)} copy(bf16[1,1600,832]{1,2,0:T(8,128)(2,1)S(1)} %fusion.92) | data formatting | bytes 5324800
  608.8 4.7 copy.332
  614.7 2.5 fusion.93
  617.2 14.5 %copy.244 = bf16[1,1600,832]{2,0,1:T(2,128)(2,1)} copy(bf16[1,1600,832]{1,2,0:T(8,128)(2,1)} %fusion.93) | data formatting | bytes 5324800
  631.7 4.6 copy.331
  636.6 2.5 fusion.91
  639.1 14.4 %copy.240 = bf16[1,1600,832]{2,0,1:T(2,128)(2,1)} copy(bf16[1,1600,832]{1,2,0:T(8,128)(2,1)} %fusion.91) | data formatting | bytes 5324800
  653.5 4.6 copy.333
  664.7 4.8 copy.229
  673.1 3.4 fusion.90
  679.4 8.6 reduce-scatter.26.cloned.1.call-done
  690.7 35.9 %reduce-scatter.22.cloned.1.call-done = bf16[400,832]{1,0:T(8,128)(2,1)} async-done(((bf16[1600,832]{1,0:T(8,128)(2,1)}), bf16[400,832]{1,0:T(8,128)(2,1)}) %reduce-scatter.22.cloned.1.call-update) | async-done | bytes 665616
  729.4 90.1 %reduce-scatter.18.cloned.1.call-done = f32[5,1600,8]{1,0,2:T(8,128)} async-done(((f32[5,1600,128]{1,0,2:T(8,128)}), f32[5,1600,8]{1,0,2:T(8,128)}) %reduce-scatter.18.cloned.1.call-update) | async-done | bytes 256016 | tf_op jit(solution)/shard_map/reduce_scatter | solution.py:301
  821.3 56.8 %reduce-scatter.28.cloned.1.call-done = f32[8,196]{1,0:T(8,128)} async-done(((f32[128,196]{1,0:T(8,128)}), f32[8,196]{1,0:T(8,128)}) %reduce-scatter.28.cloned.1.call-update) | async-done | bytes 6288
  878.1 58.5 %reduce-scatter.20.cloned.1.call-done = f32[4,128,8]{1,2,0:T(8,128)} async-done(((f32[4,128,128]{1,2,0:T(8,128)}), f32[4,128,8]{1,2,0:T(8,128)}) %reduce-scatter.20.cloned.1.call-update) | async-done | bytes 16400 | tf_op jit(solution)/shard_map/reduce_scatter | solution.py:304
  936.6 37.6 %reduce-scatter.16.cloned.1.call-done = bf16[1,208,1600]{2,1,0:T(8,128)(2,1)} async-done(((bf16[1,832,1600]{2,1,0:T(8,128)(2,1)}), bf16[1,208,1600]{2,1,0:T(8,128)(2,1)}) %reduce-scatter.16.cloned.1.call-update) | async-done | bytes 665616 | tf_op jit(solution)/shard_map/reduce_scatter | solution.py:296
  (424 shorter events, 270.9 us)
Async XLA Ops:
  7.2 154.6 %all-gather.2.cloned.1.call-start = ((), (), s32[]{:S(2)}) async-start(), calls=%async_computation.7 | async-start | bytes 2263040 | tf_op jit(solution)/shard_map/all_gather | solution.py:136
  7.9 211.6 %all-reduce.13.cloned.1.call-start = ((), (), s32[]{:S(2)}) async-start(), calls=%async_computation.16 | async-start | bytes 262144 | tf_op jit(solution)/shard_map/psum | solution.py:20
  32.3 3.0 copy-start
  42.5 10.5 %collective-permute-start = (f32[1,32,1600]{2,1,0:T(8,128)S(1)}, f32[1,32,1600]{2,1,0:T(8,128)S(1)}, u32[]{:S(2)}, u32[]{:S(2)}) collective-permute-start(f32[1,32,1600]{2,1,0:T(8,128)S(1)} %get-tuple-element.1302), channel_id=1, source_target_pairs={{0,4},{4,8},{8,12},{1,5},{5,9},{9,13},{2,6},{6,10},{10,14},{3,7},{... | collective-permute-start | bytes 614408 | tf_op jit(solution)/shard_map/while/body/eval_jaxpr/ppermute | solution.py:15
  55.0 3.0 copy-start
  65.1 9.2 collective-permute-start
  76.2 3.0 copy-start
  86.4 8.3 collective-permute-start
  96.6 3.0 copy-start
  106.8 7.7 collective-permute-start
  116.2 18.1 %collective-permute-start = (f32[1,32,1600]{2,1,0:T(8,128)S(1)}, f32[1,32,1600]{2,1,0:T(8,128)S(1)}, u32[]{:S(2)}, u32[]{:S(2)}) collective-permute-start(f32[1,32,1600]{2,1,0:T(8,128)S(1)} %get-tuple-element.1302), channel_id=1, source_target_pairs={{0,4},{4,8},{8,12},{1,5},{5,9},{9,13},{2,6},{6,10},{10,14},{3,7},{... | collective-permute-start | bytes 614408 | tf_op jit(solution)/shard_map/while/body/eval_jaxpr/ppermute | solution.py:15
  136.1 7.7 collective-permute-start
  145.5 16.2 %collective-permute-start = (f32[1,32,1600]{2,1,0:T(8,128)S(1)}, f32[1,32,1600]{2,1,0:T(8,128)S(1)}, u32[]{:S(2)}, u32[]{:S(2)}) collective-permute-start(f32[1,32,1600]{2,1,0:T(8,128)S(1)} %get-tuple-element.1302), channel_id=1, source_target_pairs={{0,4},{4,8},{8,12},{1,5},{5,9},{9,13},{2,6},{6,10},{10,14},{3,7},{... | collective-permute-start | bytes 614408 | tf_op jit(solution)/shard_map/while/body/eval_jaxpr/ppermute | solution.py:15
  161.7 8.3 copy-start.18
  161.7 8.3 copy-start.20
  161.7 57.7 %copy-start.16 = (s32[4,1,384]{2,1,0:T(1,128)S(1)}, s32[4,1,384]{2,1,0:T(1,128)}, u32[]{:S(2)}) copy-start(s32[4,1,384]{2,1,0:T(1,128)} %param.23) | copy-start | bytes 18436
  161.7 57.7 %copy-start.17 = (s32[4,1,384]{2,1,0:T(1,128)S(1)}, s32[4,1,384]{2,1,0:T(1,128)}, u32[]{:S(2)}) copy-start(s32[4,1,384]{2,1,0:T(1,128)} %param.24) | copy-start | bytes 18436
  161.8 57.7 %copy-start.19 = (f32[4,1,384]{2,1,0:T(1,128)S(1)}, f32[4,1,384]{2,1,0:T(1,128)}, u32[]{:S(2)}) copy-start(f32[4,1,384]{2,1,0:T(1,128)} %param.25) | copy-start | bytes 18436
  170.0 134.6 %all-reduce.11.cloned.1.call-start = ((), (), s32[]{:S(2)}) async-start(), calls=%async_computation.8 | async-start | bytes 262144 | tf_op jit(solution)/shard_map/psum | solution.py:20
  224.3 3.7 copy-start.10
  226.0 450.6 %reduce-scatter.24.cloned.1.call-start = ((), (), s32[]{:S(2)}) async-start(), calls=%async_computation.13 | async-start | bytes 3584000
  304.6 2.7 copy-start.12
  318.8 1.3 copy-start.4
  318.8 6.8 collective-permute-start.1
  328.8 1.3 copy-start.4
  328.8 6.8 collective-permute-start.1
  338.8 1.3 copy-start.4
  338.9 93.1 %collective-permute-start.1 = (bf16[1,32,1600]{2,1,0:T(8,128)(2,1)}, bf16[1,32,1600]{2,1,0:T(8,128)(2,1)S(1)}, u32[]{:S(2)}, u32[]{:S(2)}) collective-permute-start(bf16[1,32,1600]{2,1,0:T(8,128)(2,1)} %get-tuple-element.1167), channel_id=1, source_target_pairs={{4,0},{8,4},{12,8},{5,1},{9,5},{13,9},{6,2},{10,6},{14,10},{7,3},{... | collective-permute-start | bytes 307208 | tf_op jit(solution)/shard_map/while/body/eval_jaxpr/ppermute | solution.py:15
  433.8 3.7 copy-start.1
  437.6 3.2 copy-start.3
  458.3 2.9 copy-start.2
  461.2 3.8 copy-start.7
  461.3 3.8 copy-start.8
  465.1 1.3 copy-start.4
  465.1 7.6 collective-permute-start.1
  474.6 3.7 copy-start.1
  478.3 3.2 copy-start.3
  499.1 2.9 copy-start.2
  502.0 3.8 copy-start.7
  502.0 3.8 copy-start.8
  505.8 1.3 copy-start.4
  505.9 7.6 collective-permute-start.1
  515.3 3.7 copy-start.1
  519.0 3.2 copy-start.3
  539.8 2.9 copy-start.2
  542.7 3.8 copy-start.7
  542.7 3.8 copy-start.8
  546.6 1.3 copy-start.4
  546.6 7.6 collective-permute-start.1
  556.0 3.7 copy-start.1
  559.8 3.2 copy-start.3
  580.5 2.9 copy-start.2
  583.5 3.8 copy-start.7
  583.5 3.8 copy-start.8
  587.3 1.3 copy-start.4
  587.3 7.0 collective-permute-start.1
  613.5 74.4 %reduce-scatter.26.cloned.1.call-start = ((), (), s32[]{:S(2)}) async-start(), calls=%async_computation.14 | async-start | bytes 3584000
  636.4 90.3 %reduce-scatter.22.cloned.1.call-start = ((), (), s32[]{:S(2)}) async-start(), calls=%async_computation.12 | async-start | bytes 3584000
  658.1 6.5 copy-start.11
  658.2 161.4 %reduce-scatter.18.cloned.1.call-start = ((), (), s32[]{:S(2)}) async-start(), calls=%async_computation.10 | async-start | bytes 7241728 | tf_op jit(solution)/shard_map/reduce_scatter | solution.py:301
  669.5 3.6 copy-start.9
  669.5 208.6 %reduce-scatter.28.cloned.1.call-start = ((), (), s32[]{:S(2)}) async-start(), calls=%async_computation.15 | async-start | bytes 139264
  671.2 265.4 %reduce-scatter.20.cloned.1.call-start = ((), (), s32[]{:S(2)}) async-start(), calls=%async_computation.11 | async-start | bytes 278528 | tf_op jit(solution)/shard_map/reduce_scatter | solution.py:304
  673.0 301.2 %reduce-scatter.16.cloned.1.call-start = ((), (), s32[]{:S(2)}) async-start(), calls=%async_computation.9 | async-start | bytes 3461120 | tf_op jit(solution)/shard_map/reduce_scatter | solution.py:296
  (3 other events, 3.2 us)
Sparse Core Ops, SparseCore 0:
  10.2 44.1 all-gather.1
  170.1 45.8 all-reduce.12
  226.1 78.4 all-reduce.10
  613.6 35.4 reduce-scatter.23
  651.7 36.2 reduce-scatter.25
  690.3 36.2 reduce-scatter.21
  731.1 88.3 reduce-scatter.17
  823.6 54.5 reduce-scatter.27
  882.2 54.3 reduce-scatter.19
  939.6 34.5 reduce-scatter.15
where the time goes:
time: 987 us; the launch traced here: 981 us
  waiting for transfers between devices  475 us (48%)
  matrix products  149 us (15%)
  local copies, waits for them, and re-layouts  142 us (14%)
  other arithmetic  88.3 us (9%)
  starting transfers between devices  56.4 us (6%)
  blocking collectives  49.4 us (5%)
  between operations  19.4 us (2%)
    ppermute x14, waiting for transfers between devices, passed_along(): return lax.ppermute(block, axis, route)  111 us
    unnamed x14, waiting for transfers between devices  102 us
    reduce_scatter x1, waiting for transfers between devices, on_device(): lax.psum_scatter(grad_reassemble.astype(jnp.float32), ('section', 'dp'),...  90.1 us
    unnamed x43, local copies, waits for them, and re-layouts  85.7 us
    psum x2, waiting for transfers between devices, broadcast(): return lax.psum(kept, axis)  75.9 us
    select_n x42, other arithmetic, put_slot(): return jnp.where(active, updated, store_array)  65.6 us
    reduce_scatter x1, waiting for transfers between devices, on_device(): lax.psum_scatter(grad_merging.astype(jnp.float32), ('section', 'dp'), sca...  58.5 us
    ppermute x14, starting transfers between devices, passed_along(): return lax.ppermute(block, axis, route)  55.6 us
  transfers between devices with their start and end apart: 24, of which 20 were waited for; matrix products, arithmetic and copies ran while one was open for 20% of the time, Pallas kernels for 0%

commit v1 on v0

--- a/solution.py
+++ b/solution.py
@@ -7,6 +7,28 @@
 HEADS = 13
 NHOOK = 4
 EPS = 1e-06
+
+
+def joined_along(tiles, dim):
+    shape = list(tiles.shape[1:])
+    shape[dim] *= tiles.shape[0]
+    return jnp.moveaxis(tiles, 0, dim).reshape(shape)
+
+
+def gather_around(shard, axis, dim):
+    size = lax.axis_size(axis)
+    pairs = [(i, (i + 1) % size) for i in range(size)]
+    back = [(b, a) for a, b in pairs]
+    lower, upper = ([], [])
+    for step in range(size - 1):
+        if step % 2 == 0:
+            lower.append(lax.ppermute(lower[-1] if lower else shard, axis, pairs))
+        else:
+            upper.append(lax.ppermute(upper[-1] if upper else shard, axis, back))
+    parts = jnp.stack([*lower[::-1], shard, *upper])
+    shift = lax.axis_index(axis) - len(lower)
+    parts = parts[(jnp.arange(size) - shift) % size]
+    return joined_along(parts, dim)
 
 
 def passed_along(block, axis, distance):
@@ -135,7 +157,7 @@
     full_reassemble, full_merging, full_predict = (
         lax.all_gather(reassemble, ("section", "dp"), axis=2, tiled=True),
         lax.all_gather(merging, ("section", "dp"), axis=2, tiled=True),
-        lax.all_gather(predict, ("section", "dp"), axis=0, tiled=True),
+        gather_around(predict, ("section", "dp"), 0),
     )
     zero_nudges = jnp.zeros((3, token_rows, inner_width), jnp.bfloat16)
     zero_rows = jnp.zeros(tokens.shape[1:], jnp.float32)

time: 987 us -> 1040 us (1.054)
  waiting for transfers between devices: 475 us -> 529 us
  blocking collectives: 49.4 us -> 20.1 us
  starting transfers between devices: 56.4 us -> 84.3 us
    psum x2, waiting for transfers between devices: 75.9 us -> 126 us  [broadcast(): return lax.psum(kept, axis)]
    all_gather x1 -> x0, blocking collectives: 31.5 us -> none  [on_device(): lax.all_gather(predict, ('section', 'dp'), axis=0, tiled=True)]
    ppermute x0 -> x15, starting transfers between devices: none -> 28.1 us  [the longest x7 27.6 us: gather_around(): upper.append(lax.ppermute(upper[-1] if upper else shard, axis, back))]
    ppermute x0 -> x15, waiting for transfers between devices: none -> 11.5 us  [the longest x8 10.4 us: gather_around(): lower.append(lax.ppermute(lower[-1] if lower else shard, axis, pairs))]
    unnamed x43 -> x62, local copies, waits for them, and re-layouts: 85.7 us -> 86.9 us
  transfers between devices with their start and end apart: 24 -> 39, of which waited for: 20 -> 29; matrix products, arithmetic and copies ran while one was open for 20% -> 19% of each run, Pallas kernels for 0% -> 0%
where the time goes in v1:
time: 1040 us; the launch traced here: 1030 us
  waiting for transfers between devices  529 us (51%)
  matrix products  149 us (14%)
  local copies, waits for them, and re-layouts  143 us (14%)
  other arithmetic  88.3 us (8%)
  starting transfers between devices  84.3 us (8%)
  blocking collectives  20.1 us (2%)
  between operations  19.3 us (2%)
    psum x2, waiting for transfers between devices, broadcast(): return lax.psum(kept, axis)  126 us
    ppermute x14, waiting for transfers between devices, passed_along(): return lax.ppermute(block, axis, route)  104 us
    unnamed x14, waiting for transfers between devices  102 us
    reduce_scatter x1, waiting for transfers between devices, on_device(): lax.psum_scatter(grad_reassemble.astype(jnp.float32), ('section', 'dp'),...  90.2 us
    unnamed x62, local copies, waits for them, and re-layouts  86.9 us
    select_n x42, other arithmetic, put_slot(): return jnp.where(active, updated, store_array)  65.6 us
    reduce_scatter x1, waiting for transfers between devices, on_device(): lax.psum_scatter(grad_merging.astype(jnp.float32), ('section', 'dp'), sca...  58.5 us
    ppermute x14, starting transfers between devices, passed_along(): return lax.ppermute(block, axis, route)  55.4 us
  transfers between devices with their start and end apart: 39, of which 29 were waited for; matrix products, arithmetic and copies ran while one was open for 19% of the time, Pallas kernels for 0%

profile of v1, /device:TPU:0, one launch (start us, length us, event | category | flops | bytes accessed | tf_op | source)
XLA Modules:
  0.0 1034.8 jit_solution(6327592184322416767)
XLA Ops:
  7.7 6.5 collective-permute-done.2
  14.2 4.4 collective-permute-start.10
  20.2 4.4 collective-permute-start.11
  25.9 4.4 collective-permute-start.12
  32.2 4.4 collective-permute-start.13
  38.6 4.5 collective-permute-start.14
  44.3 4.4 collective-permute-start.15
  48.8 20.1 %all_gather.7 = bf16[4,128,128]{1,0,2:T(4,128)(2,1)} all-gather(bf16[4,128,8]{1,0,2:T(4,128)(2,1)S(1)} %copy.220), channel_id=1, replica_groups=mesh['group'=2,'section'=4,'dp'=4] {'section','dp'}, dimensions={2}, use_global_device_ids=true | all-gather | bytes 139264 | tf_op jit(solution)/shard_map/all_gather | solution.py:159
  73.1 4.3 copy.218
  77.3 5.3 copy.219
  82.6 5.3 copy.217
  90.7 124.5 %while.42 = (s32[]{:T(128)}, f32[1,32,1600]{2,1,0:T(8,128)S(1)}, f32[4,1,32,1600]{3,2,1,0:T(8,128)}, bf16[4,1,32,1600]{3,2,1,0:T(8,128)(2,1)}, s32[]{:T(128)}, /...) while((s32[]{:T(128)}, f32[1,32,1600]{2,1,0:T(8,128)S(1)}, ...), condition=%wide.region_6.7_spmd, body=%wide.region_0.6_spmd.sunk | while | flops 344828992 | bytes 25776712 | solution.py:186
  92.4 10.4 %conditional.7 = (f32[1,32,1600]{2,1,0:T(8,128)S(1)}) conditional(s32[]{:T(128)} %convert_element_type.926, f32[1,32,1600]{2,1,0:T(8,128)S(1)} %get-tuple-element.1335, (f32[1,32,1600]{2,1,0:T(8,128)S(1)}, bf16[1600,832]{1,0:T(8,128)(2,1)}, bf16[1600,832]{1,0:T(8,128)(2,1)S(1)}, bf16[1600,832]{1,0:T(8,128)(2,1)}, bf16[832,1600]{1,0:T(8,128)(2,1)}) %tuple.182), branch_computations={%region_1.1_spmd, %region_2.5_spmd} | conditional | flops 344624192 | bytes 23596836 | solution.py:180
  92.6 2.5 convolution_convert_fusion.1
  105.6 2.8 collective-permute-done
  110.2 10.4 %conditional.7 = (f32[1,32,1600]{2,1,0:T(8,128)S(1)}) conditional(s32[]{:T(128)} %convert_element_type.926, f32[1,32,1600]{2,1,0:T(8,128)S(1)} %get-tuple-element.1335, (f32[1,32,1600]{2,1,0:T(8,128)S(1)}, bf16[1600,832]{1,0:T(8,128)(2,1)}, bf16[1600,832]{1,0:T(8,128)(2,1)S(1)}, bf16[1600,832]{1,0:T(8,128)(2,1)}, bf16[832,1600]{1,0:T(8,128)(2,1)}) %tuple.182), branch_computations={%region_1.1_spmd, %region_2.5_spmd} | conditional | flops 344624192 | bytes 23596836 | solution.py:180
  110.5 2.5 convolution_convert_fusion.1
  118.3 2.3 fusion.1
  120.6 4.4 collective-permute-start
  130.2 10.4 %conditional.7 = (f32[1,32,1600]{2,1,0:T(8,128)S(1)}) conditional(s32[]{:T(128)} %convert_element_type.926, f32[1,32,1600]{2,1,0:T(8,128)S(1)} %get-tuple-element.1335, (f32[1,32,1600]{2,1,0:T(8,128)S(1)}, bf16[1600,832]{1,0:T(8,128)(2,1)}, bf16[1600,832]{1,0:T(8,128)(2,1)S(1)}, bf16[1600,832]{1,0:T(8,128)(2,1)}, bf16[832,1600]{1,0:T(8,128)(2,1)}) %tuple.182), branch_computations={%region_1.1_spmd, %region_2.5_spmd} | conditional | flops 344624192 | bytes 23596836 | solution.py:180
  130.5 2.5 convolution_convert_fusion.1
  138.3 2.3 fusion.1
  140.6 4.4 collective-permute-start
  150.1 10.4 %conditional.7 = (f32[1,32,1600]{2,1,0:T(8,128)S(1)}) conditional(s32[]{:T(128)} %convert_element_type.926, f32[1,32,1600]{2,1,0:T(8,128)S(1)} %get-tuple-element.1335, (f32[1,32,1600]{2,1,0:T(8,128)S(1)}, bf16[1600,832]{1,0:T(8,128)(2,1)}, bf16[1600,832]{1,0:T(8,128)(2,1)S(1)}, bf16[1600,832]{1,0:T(8,128)(2,1)}, bf16[832,1600]{1,0:T(8,128)(2,1)}) %tuple.182), branch_computations={%region_1.1_spmd, %region_2.5_spmd} | conditional | flops 344624192 | bytes 23596836 | solution.py:180
  150.3 2.5 convolution_convert_fusion.1
  158.2 2.3 fusion.1
  160.4 4.4 collective-permute-start
  169.9 14.8 %collective-permute-start = (f32[1,32,1600]{2,1,0:T(8,128)S(1)}, f32[1,32,1600]{2,1,0:T(8,128)S(1)}, u32[]{:S(2)}, u32[]{:S(2)}) collective-permute-start(f32[1,32,1600]{2,1,0:T(8,128)S(1)} %get-tuple-element.1488), channel_id=1, source_target_pairs={{0,4},{4,8},{8,12},{1,5},{5,9},{9,13},{2,6},{6,10},{10,14},{3,7},{... | collective-permute-start | bytes 614408 | tf_op jit(solution)/shard_map/while/body/eval_jaxpr/ppermute | solution.py:37
  189.7 4.4 collective-permute-start
  199.2 12.7 %collective-permute-start = (f32[1,32,1600]{2,1,0:T(8,128)S(1)}, f32[1,32,1600]{2,1,0:T(8,128)S(1)}, u32[]{:S(2)}, u32[]{:S(2)}) collective-permute-start(f32[1,32,1600]{2,1,0:T(8,128)S(1)} %get-tuple-element.1488), channel_id=1, source_target_pairs={{0,4},{4,8},{8,12},{1,5},{5,9},{9,13},{2,6},{6,10},{10,14},{3,7},{... | collective-permute-start | bytes 614408 | tf_op jit(solution)/shard_map/while/body/eval_jaxpr/ppermute | solution.py:37
  223.6 47.8 %all-reduce.13.cloned.1.call-done = (bf16[128,128]{1,0:T(8,128)(2,1)}, bf16[128,128]{1,0:T(8,128)(2,1)}, bf16[128,128]{1,0:T(8,128)(2,1)}, bf16[128,128]{1,0:T(8,128)(2,1)}) async-done(((bf16[128,128]{1,0:T(8,128)(2,1)}, bf16[128,128]{1,0:T(8,128)(2,1)}, bf16[128,128]{1,0:T(8,128)(2,1)}, bf16[128,128]{1,0:T(8,128)(2,1)}), (bf16[128,128]{1,0:T(8,128)(2,1)}, bf16[128,128]{1,0:T(8,128)(2,1)}, ...) | async-done | bytes 131088 | tf_op jit(solution)/shard_map/psum | solution.py:42
  271.4 4.9 conditional.3
  280.5 77.7 %all-reduce.11.cloned.1.call-done = bf16[4,128,128]{2,1,0:T(8,128)(2,1)} async-done(((bf16[4,128,128]{2,1,0:T(8,128)(2,1)}), bf16[4,128,128]{2,1,0:T(8,128)(2,1)}) %all-reduce.11.cloned.1.call-update) | async-done | bytes 131088 | tf_op jit(solution)/shard_map/psum | solution.py:42
  364.5 2.3 copy.226
  369.3 278.7 %while.43 = (s32[]{:T(128)}, f32[1,32,1600]{2,1,0:T(8,128)S(1)}, bf16[4,3,32,832]{3,2,0,1:T(8,128)(2,1)}, bf16[4,32,1600]{2,1,0:T(8,128)(2,1)}, bf16[4,32,832]{2...) while((s32[]{:T(128)}, f32[1,32,1600]{2,1,0:T(8,128)S(1)}, ...), condition=%wide.region_24.25_spmd.clone, body=%wide.region_16.24_spmd.clone.sunk | while | flops 608857152 | bytes 61259056 | solution.py:294
  398.4 87.2 %collective-permute-done.1 = bf16[1,32,1600]{2,1,0:T(8,128)(2,1)S(1)} collective-permute-done((bf16[1,32,1600]{2,1,0:T(8,128)(2,1)}, bf16[1,32,1600]{2,1,0:T(8,128)(2,1)S(1)}, u32[]{:S(2)}, u32[]{:S(2)}) %collective-permute-start.1) | collective-permute-done | bytes 102432 | tf_op jit(solution)/shard_map/while/body/eval_jaxpr/ppermute | solution.py:37
  487.4 31.3 %conditional.8 = (bf16[1,32,1600]{2,1,0:T(8,128)(2,1)}, bf16[1,3,32,832]{3,2,1,0:T(8,128)(2,1)S(1)}, bf16[1,32,1600]{2,1,0:T(8,128)(2,1)}, bf16[1,32,832]{2,1,0:T(8,128)(2,1)S(1)}) conditional(s32[]{:T(128)} %convert_element_type.927, () %tuple.185, (f32[1,32,1600]{2,1,0:T(8,128)S(1)}, bf16[832,1600]{1,0:T(8,128)(2,1)}, ...), branch_computations={%region_17.17_spmd, %region_18.23_spmd} | conditional | flops 608443456 | bytes 57541052 | solution.py:273
  488.7 2.5 convolution_convert_fusion.13
  512.0 2.9 convolution_convert_fusion.5
  528.2 31.3 %conditional.8 = (bf16[1,32,1600]{2,1,0:T(8,128)(2,1)}, bf16[1,3,32,832]{3,2,1,0:T(8,128)(2,1)S(1)}, bf16[1,32,1600]{2,1,0:T(8,128)(2,1)}, bf16[1,32,832]{2,1,0:T(8,128)(2,1)S(1)}) conditional(s32[]{:T(128)} %convert_element_type.927, () %tuple.185, (f32[1,32,1600]{2,1,0:T(8,128)S(1)}, bf16[832,1600]{1,0:T(8,128)(2,1)}, ...), branch_computations={%region_17.17_spmd, %region_18.23_spmd} | conditional | flops 608443456 | bytes 57541052 | solution.py:273
  529.4 2.5 convolution_convert_fusion.13
  552.7 2.9 convolution_convert_fusion.5
  568.9 31.3 %conditional.8 = (bf16[1,32,1600]{2,1,0:T(8,128)(2,1)}, bf16[1,3,32,832]{3,2,1,0:T(8,128)(2,1)S(1)}, bf16[1,32,1600]{2,1,0:T(8,128)(2,1)}, bf16[1,32,832]{2,1,0:T(8,128)(2,1)S(1)}) conditional(s32[]{:T(128)} %convert_element_type.927, () %tuple.185, (f32[1,32,1600]{2,1,0:T(8,128)S(1)}, bf16[832,1600]{1,0:T(8,128)(2,1)}, ...), branch_computations={%region_17.17_spmd, %region_18.23_spmd} | conditional | flops 608443456 | bytes 57541052 | solution.py:273
  570.1 2.5 convolution_convert_fusion.13
  593.4 2.9 convolution_convert_fusion.5
  609.7 31.3 %conditional.8 = (bf16[1,32,1600]{2,1,0:T(8,128)(2,1)}, bf16[1,3,32,832]{3,2,1,0:T(8,128)(2,1)S(1)}, bf16[1,32,1600]{2,1,0:T(8,128)(2,1)}, bf16[1,32,832]{2,1,0:T(8,128)(2,1)S(1)}) conditional(s32[]{:T(128)} %convert_element_type.927, () %tuple.185, (f32[1,32,1600]{2,1,0:T(8,128)S(1)}, bf16[832,1600]{1,0:T(8,128)(2,1)}, ...), branch_computations={%region_17.17_spmd, %region_18.23_spmd} | conditional | flops 608443456 | bytes 57541052 | solution.py:273
  610.9 2.5 convolution_convert_fusion.13
  634.2 2.9 convolution_convert_fusion.5
  650.0 12.4 %copy.245 = bf16[1,1600,832]{2,0,1:T(2,128)(2,1)} copy(bf16[1,1600,832]{1,2,0:T(8,128)(2,1)S(1)} %fusion.97) | data formatting | bytes 5324800
  662.4 4.7 copy.335
  668.3 2.5 fusion.98
  670.8 14.5 %copy.247 = bf16[1,1600,832]{2,0,1:T(2,128)(2,1)} copy(bf16[1,1600,832]{1,2,0:T(8,128)(2,1)} %fusion.98) | data formatting | bytes 5324800
  685.3 4.7 copy.334
  690.2 2.4 fusion.96
  692.7 14.3 %copy.243 = bf16[1,1600,832]{2,0,1:T(2,128)(2,1)} copy(bf16[1,1600,832]{1,2,0:T(8,128)(2,1)} %fusion.96) | data formatting | bytes 5324800
  707.0 4.6 copy.336
  718.2 4.8 copy.232
  726.6 3.4 fusion.95
  732.9 8.6 reduce-scatter.26.cloned.1.call-done
  744.3 35.8 %reduce-scatter.22.cloned.1.call-done = bf16[400,832]{1,0:T(8,128)(2,1)} async-done(((bf16[1600,832]{1,0:T(8,128)(2,1)}), bf16[400,832]{1,0:T(8,128)(2,1)}) %reduce-scatter.22.cloned.1.call-update) | async-done | bytes 665616
  783.0 90.2 %reduce-scatter.18.cloned.1.call-done = f32[5,1600,8]{1,0,2:T(8,128)} async-done(((f32[5,1600,128]{1,0,2:T(8,128)}), f32[5,1600,8]{1,0,2:T(8,128)}) %reduce-scatter.18.cloned.1.call-update) | async-done | bytes 256016 | tf_op jit(solution)/shard_map/reduce_scatter | solution.py:323
  874.9 56.8 %reduce-scatter.28.cloned.1.call-done = f32[8,196]{1,0:T(8,128)} async-done(((f32[128,196]{1,0:T(8,128)}), f32[8,196]{1,0:T(8,128)}) %reduce-scatter.28.cloned.1.call-update) | async-done | bytes 6288
  931.8 58.5 %reduce-scatter.20.cloned.1.call-done = f32[4,128,8]{1,2,0:T(8,128)} async-done(((f32[4,128,128]{1,2,0:T(8,128)}), f32[4,128,8]{1,2,0:T(8,128)}) %reduce-scatter.20.cloned.1.call-update) | async-done | bytes 16400 | tf_op jit(solution)/shard_map/reduce_scatter | solution.py:326
  990.3 37.6 %reduce-scatter.16.cloned.1.call-done = bf16[1,208,1600]{2,1,0:T(8,128)(2,1)} async-done(((bf16[1,832,1600]{2,1,0:T(8,128)(2,1)}), bf16[1,208,1600]{2,1,0:T(8,128)(2,1)}) %reduce-scatter.16.cloned.1.call-update) | async-done | bytes 665616 | tf_op jit(solution)/shard_map/reduce_scatter | solution.py:318
  (474 shorter events, 292.5 us)
Async XLA Ops:
  7.2 208.1 %all-gather.2.cloned.1.call-start = ((), (), s32[]{:S(2)}) async-start(), calls=%async_computation.7 | async-start | bytes 2263040 | tf_op jit(solution)/shard_map/all_gather | solution.py:158
  7.2 7.0 collective-permute-start.2
  14.2 5.7 collective-permute-start.3
  14.2 6.0 collective-permute-start.10
  19.9 5.7 collective-permute-start.4
  20.2 5.7 collective-permute-start.11
  25.6 5.7 collective-permute-start.5
  25.7 245.7 %all-reduce.13.cloned.1.call-start = ((), (), s32[]{:S(2)}) async-start(), calls=%async_computation.16 | async-start | bytes 262144 | tf_op jit(solution)/shard_map/psum | solution.py:42
  25.9 6.3 collective-permute-start.12
  31.4 5.7 collective-permute-start.6
  32.2 6.4 collective-permute-start.13
  37.1 5.9 collective-permute-start.7
  38.6 5.8 collective-permute-start.14
  43.0 5.7 collective-permute-start.8
  44.3 43.5 %collective-permute-start.15 = (bf16[8,196]{1,0:T(8,128)(2,1)S(1)}, bf16[8,196]{1,0:T(8,128)(2,1)S(1)}, u32[]{:S(2)}, u32[]{:S(2)}) collective-permute-start(bf16[8,196]{1,0:T(8,128)(2,1)S(1)} %collective-permute-done.14), channel_id=1, source_target_pairs={{1,0},{2,1},{3,2},{4,3},{5,4},{6,5},{7,6},{8,7},{9,8},{10,9},{11,1... | collective-permute-start | bytes 9416 | tf_op jit(solution)/shard_map/ppermute | solution.py:27
  48.8 40.1 %collective-permute-start.9 = (bf16[8,196]{1,0:T(8,128)(2,1)S(1)}, bf16[8,196]{1,0:T(8,128)(2,1)S(1)}, u32[]{:S(2)}, u32[]{:S(2)}) collective-permute-start(bf16[8,196]{1,0:T(8,128)(2,1)S(1)} %collective-permute-done.8), channel_id=1, source_target_pairs={{0,1},{1,2},{2,3},{3,4},{4,5},{5,6},{6,7},{7,8},{8,9},{9,10},{10,1... | collective-permute-start | bytes 9416 | tf_op jit(solution)/shard_map/ppermute | solution.py:25
  82.6 6.4 copy-start.20
  87.9 135.7 %collective-permute-start.16 = (bf16[8,196]{1,0:T(8,128)(2,1)S(1)}, bf16[8,196]{1,0:T(8,128)(2,1)S(1)}, u32[]{:S(2)}, u32[]{:S(2)}) collective-permute-start(bf16[8,196]{1,0:T(8,128)(2,1)S(1)} %collective-permute-done.15), channel_id=1, source_target_pairs={{1,0},{2,1},{3,2},{4,3},{5,4},{6,5},{7,6},{8,7},{9,8},{10,9},{11,1... | collective-permute-start | bytes 9416 | tf_op jit(solution)/shard_map/ppermute | solution.py:27
  102.8 5.7 collective-permute-start
  120.6 7.9 collective-permute-start
  140.6 7.8 collective-permute-start
  160.4 7.7 collective-permute-start
  169.9 18.1 %collective-permute-start = (f32[1,32,1600]{2,1,0:T(8,128)S(1)}, f32[1,32,1600]{2,1,0:T(8,128)S(1)}, u32[]{:S(2)}, u32[]{:S(2)}) collective-permute-start(f32[1,32,1600]{2,1,0:T(8,128)S(1)} %get-tuple-element.1488), channel_id=1, source_target_pairs={{0,4},{4,8},{8,12},{1,5},{5,9},{9,13},{2,6},{6,10},{10,14},{3,7},{... | collective-permute-start | bytes 614408 | tf_op jit(solution)/shard_map/while/body/eval_jaxpr/ppermute | solution.py:37
  189.7 7.7 collective-permute-start
  199.2 16.0 %collective-permute-start = (f32[1,32,1600]{2,1,0:T(8,128)S(1)}, f32[1,32,1600]{2,1,0:T(8,128)S(1)}, u32[]{:S(2)}, u32[]{:S(2)}) collective-permute-start(f32[1,32,1600]{2,1,0:T(8,128)S(1)} %get-tuple-element.1488), channel_id=1, source_target_pairs={{0,4},{4,8},{8,12},{1,5},{5,9},{9,13},{2,6},{6,10},{10,14},{3,7},{... | collective-permute-start | bytes 614408 | tf_op jit(solution)/shard_map/while/body/eval_jaxpr/ppermute | solution.py:37
  215.2 8.4 copy-start.16
  215.2 56.2 %copy-start.12 = (bf16[4,128,128]{1,0,2:T(4,128)(2,1)S(1)}, bf16[4,128,128]{1,0,2:T(4,128)(2,1)}, u32[]{:S(2)}) copy-start(bf16[4,128,128]{1,0,2:T(4,128)(2,1)} %all_gather.7) | copy-start | bytes 393220
  215.2 56.2 %copy-start.17 = (s32[4,1,384]{2,1,0:T(1,128)S(1)}, s32[4,1,384]{2,1,0:T(1,128)}, u32[]{:S(2)}) copy-start(s32[4,1,384]{2,1,0:T(1,128)} %param.23) | copy-start | bytes 18436
  215.2 56.2 %copy-start.18 = (s32[4,1,384]{2,1,0:T(1,128)S(1)}, s32[4,1,384]{2,1,0:T(1,128)}, u32[]{:S(2)}) copy-start(s32[4,1,384]{2,1,0:T(1,128)} %param.24) | copy-start | bytes 18436
  215.2 56.2 %copy-start.19 = (f32[4,1,384]{2,1,0:T(1,128)S(1)}, f32[4,1,384]{2,1,0:T(1,128)}, u32[]{:S(2)}) copy-start(f32[4,1,384]{2,1,0:T(1,128)} %param.25) | copy-start | bytes 18436
  223.5 134.7 %all-reduce.11.cloned.1.call-start = ((), (), s32[]{:S(2)}) async-start(), calls=%async_computation.8 | async-start | bytes 262144 | tf_op jit(solution)/shard_map/psum | solution.py:42
  276.3 3.7 copy-start.10
  277.9 452.2 %reduce-scatter.24.cloned.1.call-start = ((), (), s32[]{:S(2)}) async-start(), calls=%async_computation.13 | async-start | bytes 3584000
  372.4 6.8 collective-permute-start.1
  382.4 6.8 collective-permute-start.1
  392.4 93.2 %collective-permute-start.1 = (bf16[1,32,1600]{2,1,0:T(8,128)(2,1)}, bf16[1,32,1600]{2,1,0:T(8,128)(2,1)S(1)}, u32[]{:S(2)}, u32[]{:S(2)}) collective-permute-start(bf16[1,32,1600]{2,1,0:T(8,128)(2,1)} %get-tuple-element.1353), channel_id=1, source_target_pairs={{4,0},{8,4},{12,8},{5,1},{9,5},{13,9},{6,2},{10,6},{14,10},{7,3},{... | collective-permute-start | bytes 307208 | tf_op jit(solution)/shard_map/while/body/eval_jaxpr/ppermute | solution.py:37
  487.4 3.7 copy-start.1
  491.2 3.2 copy-start.3
  514.9 3.8 copy-start.7
  514.9 3.8 copy-start.8
  518.7 7.6 collective-permute-start.1
  528.2 3.7 copy-start.1
  531.9 3.2 copy-start.3
  555.6 3.8 copy-start.7
  555.6 3.8 copy-start.8
  559.5 7.6 collective-permute-start.1
  568.9 3.7 copy-start.1
  572.7 3.2 copy-start.3
  596.4 3.8 copy-start.7
  596.4 3.8 copy-start.8
  600.2 7.6 collective-permute-start.1
  609.7 3.7 copy-start.1
  613.4 3.2 copy-start.3
  637.1 3.8 copy-start.7
  637.1 3.8 copy-start.8
  641.0 7.0 collective-permute-start.1
  667.1 74.5 %reduce-scatter.26.cloned.1.call-start = ((), (), s32[]{:S(2)}) async-start(), calls=%async_computation.14 | async-start | bytes 3584000
  690.0 90.2 %reduce-scatter.22.cloned.1.call-start = ((), (), s32[]{:S(2)}) async-start(), calls=%async_computation.12 | async-start | bytes 3584000
  711.6 6.5 copy-start.11
  711.7 161.5 %reduce-scatter.18.cloned.1.call-start = ((), (), s32[]{:S(2)}) async-start(), calls=%async_computation.10 | async-start | bytes 7241728 | tf_op jit(solution)/shard_map/reduce_scatter | solution.py:323
  723.0 3.6 copy-start.9
  723.1 208.7 %reduce-scatter.28.cloned.1.call-start = ((), (), s32[]{:S(2)}) async-start(), calls=%async_computation.15 | async-start | bytes 139264
  724.7 265.5 %reduce-scatter.20.cloned.1.call-start = ((), (), s32[]{:S(2)}) async-start(), calls=%async_computation.11 | async-start | bytes 278528 | tf_op jit(solution)/shard_map/reduce_scatter | solution.py:326
  726.6 301.4 %reduce-scatter.16.cloned.1.call-start = ((), (), s32[]{:S(2)}) async-start(), calls=%async_computation.9 | async-start | bytes 3461120 | tf_op jit(solution)/shard_map/reduce_scatter | solution.py:318
  (20 other events, 39.5 us)
Sparse Core Ops, SparseCore 0:
  25.8 43.5 all-gather.1
  223.6 47.7 all-reduce.12
  278.0 80.1 all-reduce.10
  667.2 35.4 reduce-scatter.23
  705.3 36.2 reduce-scatter.25
  743.9 36.2 reduce-scatter.21
  784.7 88.4 reduce-scatter.17
  877.2 54.5 reduce-scatter.27
  935.9 54.3 reduce-scatter.19
  993.3 34.6 reduce-scatter.15
